TPU v7x, 512 devices: a whole 4x4x16 slice. The times are simulated.
512 devices in a mesh: blk: 64 (over y, z_lo, core), tgt: 8 (over x, z_hi).
Axes of the slice: x: 4, y: 4, z: 16 (z_hi: 2, z_lo: 8; z = z_hi * 8 + z_lo), core: 2. Of those that a mesh axis runs over, the one named last changes fastest.
Arguments:
- history: float32 [32768, 1536], P(('blk', 'tgt')), may hold values from 0 to 2
- weights: bfloat16 [64, 512, 32768], P(None, 'tgt', 'blk'), may hold values from -0.03125 to 0.03125
- delays: int32 [32, 32], replicated, may hold values from 16 to 64
- area_blocks: int32 [32], replicated, may hold values from 1 to 3, 64 in all
- potential: float32 [24, 32768], P(None, ('blk', 'tgt')), may hold values from -6 to 6
- leak: float32 [32768], P(('blk', 'tgt')), may hold values from 0.03 to 0.6
- drive: float32 [32768], P(('blk', 'tgt')), may hold values from -6 to 6
Outputs:
- rate_steps: float32 [16, 24, 32768], P(None, None, ('blk', 'tgt'))
- last_potential: float32 [24, 32768], P(None, ('blk', 'tgt'))
Inputs may be any that keep to these rules, and one draw needn't show every extreme that they name: Area a consists of area_blocks[a] consecutive blocks of 512 neurons; areas follow one another in order.
All inputs are finite; a program needn't handle non-finite values.
Results may differ from a plain program's by a relative error of at most 0.00083.
Values may be sent and summed in bfloat16 or wider, within the bound.
A program may use at most 128 MiB of HBM per device.

v0:
```python
import jax
import jax.numpy as jnp
from jax import lax
from jax.sharding import PartitionSpec as P

STEPS = 16


def cut_along(x, dim, peers):
    lengths = x.shape
    parts = x.reshape(*lengths[:dim], peers, lengths[dim] // peers, *lengths[dim + 1 :])
    return jnp.moveaxis(parts, dim, 0)


def summed_on_arrival(x, axis, dim):
    parts = cut_along(x, dim, lax.axis_size(axis))
    arrived = lax.all_to_all(parts, axis, split_axis=0, concat_axis=0, tiled=True)
    return arrived.sum(axis=0)


def block_areas(area_blocks, block_count):
    boundary = jnp.cumsum(area_blocks)
    blocks = jnp.arange(block_count, dtype=jnp.int32)
    return jnp.sum((boundary[None, :] <= blocks[:, None]).astype(jnp.int32), axis=1)


def on_device(history, weights, delays, area_blocks, potential, leak, drive):
    block_count = weights.shape[0]
    piece_width = weights.shape[1]
    columns = history.shape[1]
    trial_count = potential.shape[0]
    window_width = STEPS * trial_count
    area_of_block = block_areas(area_blocks, block_count)
    my_block = lax.axis_index("blk")
    my_area = area_of_block[my_block]
    history_low = history.astype(jnp.bfloat16)

    def window(lag_step, column):
        start = columns - lag_step * trial_count
        return lax.dynamic_slice_in_dim(column, start, window_width, 1)

    lag_steps = delays[my_area][area_of_block]
    arrived = lax.all_gather(history_low, "blk", axis=0, tiled=True)
    shard_count = arrived.shape[0] // piece_width
    shaped = arrived.reshape(shard_count, piece_width, columns)
    delayed_input = jax.vmap(window, in_axes=(0, 0))(lag_steps, shaped)
    partial_input = jnp.einsum(
        "gyw,gyt->wt", delayed_input, weights, preferred_element_type=jnp.float32
    )
    own_input = summed_on_arrival(partial_input, "tgt", 1)
    own_input = own_input.reshape(STEPS, trial_count, piece_width)

    def advance(membrane_state, synaptic):
        membrane_state = membrane_state + leak * (drive - membrane_state + synaptic)
        return (membrane_state, jax.nn.softplus(membrane_state))

    last_potential, rate_steps = lax.scan(advance, potential, own_input)
    return (rate_steps, last_potential)


def solution(mesh):
    in_specs = (
        P(("blk", "tgt"), None),
        P(None, "tgt", "blk"),
        P(),
        P(),
        P(None, ("blk", "tgt")),
        P(("blk", "tgt")),
        P(("blk", "tgt")),
    )
    out_specs = (P(None, None, ("blk", "tgt")), P(None, ("blk", "tgt")))
    return jax.shard_map(
        on_device, mesh=mesh, in_specs=in_specs, out_specs=out_specs, check_vma=False
    )
```

profile of v0, /device:TPU:32, one launch (start us, length us, event | category | flops | bytes accessed | tf_op | source)
XLA Modules:
  0.0 295.5 jit_solution(2415706052495670528)
XLA Ops:
  7.2 1.7 convert_element_type.6
  8.9 0.7 copy.26
  9.7 0.1 reduce-window.8
  9.7 0.1 reduce
  9.9 0.1 convert_reduce_fusion
  10.0 0.6 dynamic_slice.10
  12.3 0.8 gather_fusion
  13.1 135.9 %all-gather.2.cloned.1.call-done = bf16[4096,1536]{1,0:T(8,128)(2,1)} async-done(((bf16[64,1536]{1,0:T(8,128)(2,1)}), bf16[4096,1536]{1,0:T(8,128)(2,1)}) %all-gather.2.cloned.1.call-update) | async-done | bytes 12582928 | tf_op jit(solution)/shard_map/all_gather | solution.py:43
  149.0 35.0 %copy.27 = bf16[64,64,1536]{1,0,2:T(8,128)(2,1)} copy(bf16[64,64,1536]{2,1,0:T(8,128)(2,1)} %bitcast.39) | data formatting | bytes 25165824 | tf_op jit(solution)/shard_map/reshape | solution.py:45
  184.0 24.2 %gather_fusion.1 = bf16[64,64,384]{1,0,2:T(8,128)(2,1)} fusion(bf16[64,64,1536]{1,0,2:T(8,128)(2,1)} %copy.27, s32[64]{0:T(128)S(1)} %or_bitcast_fusion), kind=kCustom, calls=%fused_computation.1 | custom fusion | bytes 6292224 | tf_op jit(solution)/shard_map/vmap()/gather | solution.py:40
  208.2 12.3 %fusion.4 = f32[384,512,1]{0,1,2:T(8,128)} fusion(bf16[64,64,512]{2,1,0:T(8,128)(2,1)} %param.10, bf16[64,64,384]{1,0,2:T(8,128)(2,1)} %gather_fusion.1), kind=kOutput, calls=%fused_computation.8 | convolution fusion | flops 1610612736 | bytes 8126464 | tf_op jit(solution)/shard_map/gyw,gyt->wt/dot_general | solution.py:47
  220.5 10.0 %all-to-all-start = ((f32[8,384,64]{1,2,0:T(8,128)}), f32[8,384,64]{1,2,0:T(8,128)S(1)}, u32[]{:S(2)}, u32[]{:S(2)}) async-start(f32[8,384,64]{1,2,0:T(8,128)} %bitcast.13), calls=%async_computation | async-start | bytes 1572864 | tf_op jit(solution)/shard_map/all_to_all | solution.py:17
  230.5 47.3 %all-to-all-done = f32[8,384,64]{1,2,0:T(8,128)S(1)} async-done(((f32[8,384,64]{1,2,0:T(8,128)}), f32[8,384,64]{1,2,0:T(8,128)S(1)}, u32[]{:S(2)}, u32[]{:S(2)}) %all-to-all-start) | async-done | bytes 786464 | tf_op jit(solution)/shard_map/all_to_all | solution.py:17
  277.9 0.1 copy.30
  278.1 10.0 %while.12 = (s32[]{:T(128)}, f32[24,64]{1,0:T(8,128)S(1)}, f32[16,24,64]{2,1,0:T(8,128)}, f32[64]{0:T(128)S(1)}, f32[64]{0:T(128)S(1)}, /*index=5*/f32[16,24,64]{2,1,0:T(8,128)S(1)}, s32[]{:T(128)}) while((s32[]{:T(128)}, f32[24,64]{1,0:T(8,128)S(1)}, f32[16,24,64]{2,1,0:T(8,128)}, f32[64]{0:T(128)S(1)}, f32[64]{0:T(128)S(1)}, ...), condition=%wide.region_4.5_spmd, body=%wide.region_3.4_spmd.sunk | while | flops 15362 | bytes 31821 | solution.py:57
  278.1 0.6 fusion.11
  278.7 0.6 fusion.11
  279.3 0.6 fusion.11
  280.0 0.6 fusion.11
  280.6 0.6 fusion.11
  281.2 0.6 fusion.11
  281.8 0.6 fusion.11
  282.5 0.6 fusion.11
  283.1 0.6 fusion.11
  283.7 0.6 fusion.11
  284.3 0.6 fusion.11
  285.0 0.6 fusion.11
  285.6 0.6 fusion.11
  286.2 0.6 fusion.11
  286.8 0.6 fusion.11
  287.4 0.6 fusion.11
  288.1 0.6 copy-done.1
  (17 shorter events, 0.2 us)
Async XLA Ops:
  7.2 5.1 %copy-start = (s32[32,32]{1,0:T(8,128)S(1)}, s32[32,32]{1,0:T(8,128)}, u32[]{:S(2)}) copy-start(s32[32,32]{1,0:T(8,128)} %param.11) | copy-start | bytes 12292
  7.2 141.8 %all-gather.2.cloned.1.call-start = ((), (), s32[]{:S(2)}) async-start(), calls=%async_computation.1 | async-start | bytes 12779520 | tf_op jit(solution)/shard_map/all_gather | solution.py:43
  208.1 69.9 %copy-start.2 = (f32[24,64]{1,0:T(8,128)S(1)}, f32[24,64]{1,0:T(8,128)}, u32[]{:S(2)}) copy-start(f32[24,64]{1,0:T(8,128)} %param.13) | copy-start | bytes 18436
  208.2 69.9 %copy-start.3 = (f32[64]{0:T(128)S(1)}, f32[64]{0:T(128)}, u32[]{:S(2)}) copy-start(f32[64]{0:T(128)} %param.14) | copy-start | bytes 772
  208.2 69.9 %copy-start.4 = (f32[64]{0:T(128)S(1)}, f32[64]{0:T(128)}, u32[]{:S(2)}) copy-start(f32[64]{0:T(128)} %param.15) | copy-start | bytes 772
  220.5 57.4 %all-to-all-start = ((f32[8,384,64]{1,2,0:T(8,128)}), f32[8,384,64]{1,2,0:T(8,128)S(1)}, u32[]{:S(2)}, u32[]{:S(2)}) async-start(f32[8,384,64]{1,2,0:T(8,128)} %bitcast.13), calls=%async_computation | async-start | bytes 1572864 | tf_op jit(solution)/shard_map/all_to_all | solution.py:17
  288.1 0.6 copy-start.1
Sparse Core Ops, SparseCore 0:
  10.7 138.2 all-gather.1
where the time goes:
time: 297 us; the launch traced here: 296 us
  waiting for transfers between devices  183 us (62%)
  local copies, waits for them, and re-layouts  62 us (21%)
  between operations  15.8 us (5%)
  matrix products  12.3 us (4%)
  other arithmetic  12 us (4%)
  starting transfers between devices  10.1 us (3%)
    all_gather x1, waiting for transfers between devices, on_device(): arrived = lax.all_gather(history_low, 'blk', axis=0, tiled=True)  136 us
    all_to_all x1, waiting for transfers between devices, summed_on_arrival(): lax.all_to_all(parts, axis, split_axis=0, concat_axis=0, tiled=True)  47.3 us
    reshape x1, local copies, waits for them, and re-layouts, on_device(): shaped = arrived.reshape(shard_count, piece_width, columns)  35 us
    gather x1, local copies, waits for them, and re-layouts, window(): return lax.dynamic_slice_in_dim(column, start, window_width, 1)  24.2 us
    dot_general x1, matrix products, on_device(): jnp.einsum('gyw,gyt->wt', delayed_input, weights, preferred_element_type=...  12.3 us
    all_to_all x1, starting transfers between devices, summed_on_arrival(): lax.all_to_all(parts, axis, split_axis=0, concat_axis=0, tiled=True)  10 us
    dynamic_update_slice x16, other arithmetic, on_device(): last_potential, rate_steps = lax.scan(advance, potential, own_input)  9.98 us
  transfers between devices with their start and end apart: 2, of which 2 were waited for; matrix products, arithmetic and copies ran while one was open for 1% of the time, Pallas kernels for 0%

commit v1 on v0

--- a/solution.py
+++ b/solution.py
@@ -40,7 +40,9 @@
         return lax.dynamic_slice_in_dim(column, start, window_width, 1)
 
     lag_steps = delays[my_area][area_of_block]
-    arrived = lax.all_gather(history_low, "blk", axis=0, tiled=True)
+    arrived = jnp.concatenate(
+        lax.all_to_all(jnp.stack([history_low] * lax.axis_size("blk")), "blk", 0, 0), axis=0
+    )
     shard_count = arrived.shape[0] // piece_width
     shaped = arrived.reshape(shard_count, piece_width, columns)
     delayed_input = jax.vmap(window, in_axes=(0, 0))(lag_steps, shaped)

time: 297 us -> 697 us (2.35)
  the two profiles are of different devices: /device:TPU:32 before, /device:TPU:19 now
where the time goes in v1:
time: 697 us; the launch traced here: 696 us
  waiting for transfers between devices  575 us (82%)
  local copies, waits for them, and re-layouts  67.4 us (10%)
  starting transfers between devices  26.8 us (4%)
  matrix products  12.4 us (2%)
  other arithmetic  11.3 us (2%)
    all_to_all x1, waiting for transfers between devices, on_device(): lax.all_to_all(jnp.stack([history_low] * lax.axis_size('blk')), 'blk', 0, 0)  542 us
    all_to_all x1, local copies, waits for them, and re-layouts, on_device(): lax.all_to_all(jnp.stack([history_low] * lax.axis_size('blk')), 'blk', 0, 0)  35 us
    all_to_all x1, waiting for transfers between devices, summed_on_arrival(): lax.all_to_all(parts, axis, split_axis=0, concat_axis=0, tiled=True)  32.9 us
    gather x1, local copies, waits for them, and re-layouts, window(): return lax.dynamic_slice_in_dim(column, start, window_width, 1)  24.2 us
    all_to_all x1, starting transfers between devices, on_device(): lax.all_to_all(jnp.stack([history_low] * lax.axis_size('blk')), 'blk', 0, 0)  16.8 us
  transfers between devices with their start and end apart: 2, of which 2 were waited for; matrix products, arithmetic and copies ran while one was open for 0% of the time, Pallas kernels for 0%

profile of v1, /device:TPU:19, one launch (start us, length us, event | category | flops | bytes accessed | tf_op | source)
XLA Modules:
  0.0 695.6 jit_solution(12048705581603764835)
XLA Ops:
  0.6 1.0 convert_element_type.6
  1.7 6.1 stack.2
  7.8 16.8 %all-to-all-start = ((bf16[64,64,1536]{2,1,0:T(8,128)(2,1)}), bf16[64,64,1536]{2,1,0:T(8,128)(2,1)}, u32[]{:S(2)}, u32[]{:S(2)}) async-start(bf16[64,64,1536]{2,1,0:T(8,128)(2,1)} %stack.2), calls=%async_computation | async-start | bytes 25165824 | tf_op jit(solution)/shard_map/all_to_all | solution.py:44
  24.7 0.1 reduce
  24.8 0.1 convert_reduce_fusion
  24.9 0.6 dynamic_slice.10
  27.5 0.8 gather_fusion
  28.3 542.0 %all-to-all-done = bf16[64,64,1536]{2,1,0:T(8,128)(2,1)} async-done(((bf16[64,64,1536]{2,1,0:T(8,128)(2,1)}), bf16[64,64,1536]{2,1,0:T(8,128)(2,1)}, u32[]{:S(2)}, u32[]{:S(2)}) %all-to-all-start) | async-done | bytes 12582944 | tf_op jit(solution)/shard_map/all_to_all | solution.py:44
  570.3 35.0 %copy.27 = bf16[64,64,1536]{1,0,2:T(8,128)(2,1)} copy(bf16[64,64,1536]{2,1,0:T(8,128)(2,1)} %all-to-all-done) | data formatting | bytes 25165824 | tf_op jit(solution)/shard_map/all_to_all | solution.py:44
  605.3 24.2 %gather_fusion.1 = bf16[64,64,384]{1,0,2:T(8,128)(2,1)} fusion(bf16[64,64,1536]{1,0,2:T(8,128)(2,1)} %copy.27, s32[64]{0:T(128)S(1)} %or_bitcast_fusion), kind=kCustom, calls=%fused_computation.1 | custom fusion | bytes 6292224 | tf_op jit(solution)/shard_map/vmap()/gather | solution.py:40
  629.5 12.4 %fusion.4 = f32[384,512,1]{0,1,2:T(8,128)} fusion(bf16[64,64,512]{2,1,0:T(8,128)(2,1)} %param.10, bf16[64,64,384]{1,0,2:T(8,128)(2,1)} %gather_fusion.1), kind=kOutput, calls=%fused_computation.8 | convolution fusion | flops 1610612736 | bytes 8126464 | tf_op jit(solution)/shard_map/gyw,gyt->wt/dot_general | solution.py:49
  641.9 10.0 %all-to-all-start.1 = ((f32[8,384,64]{1,2,0:T(8,128)}), f32[8,384,64]{1,2,0:T(8,128)S(1)}, u32[]{:S(2)}, u32[]{:S(2)}) async-start(f32[8,384,64]{1,2,0:T(8,128)} %bitcast.12), calls=%async_computation.1 | async-start | bytes 1572864 | tf_op jit(solution)/shard_map/all_to_all | solution.py:17
  651.9 32.9 %all-to-all-done.1 = f32[8,384,64]{1,2,0:T(8,128)S(1)} async-done(((f32[8,384,64]{1,2,0:T(8,128)}), f32[8,384,64]{1,2,0:T(8,128)S(1)}, u32[]{:S(2)}, u32[]{:S(2)}) %all-to-all-start.1) | async-done | bytes 786464 | tf_op jit(solution)/shard_map/all_to_all | solution.py:17
  684.8 0.1 copy.30
  685.0 10.0 %while.12 = (s32[]{:T(128)}, f32[24,64]{1,0:T(8,128)S(1)}, f32[16,24,64]{2,1,0:T(8,128)}, f32[64]{0:T(128)S(1)}, f32[64]{0:T(128)S(1)}, /*index=5*/f32[16,24,64]{2,1,0:T(8,128)S(1)}, s32[]{:T(128)}) while((s32[]{:T(128)}, f32[24,64]{1,0:T(8,128)S(1)}, f32[16,24,64]{2,1,0:T(8,128)}, f32[64]{0:T(128)S(1)}, f32[64]{0:T(128)S(1)}, ...), condition=%wide.region_4.5_spmd, body=%wide.region_3.4_spmd.sunk | while | flops 15362 | bytes 31821 | solution.py:59
  685.0 0.6 fusion.11
  685.6 0.6 fusion.11
  686.2 0.6 fusion.11
  686.9 0.6 fusion.11
  687.5 0.6 fusion.11
  688.1 0.6 fusion.11
  688.7 0.6 fusion.11
  689.4 0.6 fusion.11
  690.0 0.6 fusion.11
  690.6 0.6 fusion.11
  691.2 0.6 fusion.11
  691.8 0.6 fusion.11
  692.5 0.6 fusion.11
  693.1 0.6 fusion.11
  693.7 0.6 fusion.11
  694.3 0.6 fusion.11
  695.0 0.6 copy-done.1
  (19 shorter events, 0.2 us)
Async XLA Ops:
  0.6 26.8 %copy-start = (s32[32,32]{1,0:T(8,128)S(1)}, s32[32,32]{1,0:T(8,128)}, u32[]{:S(2)}) copy-start(s32[32,32]{1,0:T(8,128)} %param.11) | copy-start | bytes 12292
  7.8 16.8 %copy-start.5 = (s32[32]{0:T(128)S(1)}, s32[32]{0:T(128)}, u32[]{:S(2)}) copy-start(s32[32]{0:T(128)} %param.12) | copy-start | bytes 388
  7.8 562.6 %all-to-all-start = ((bf16[64,64,1536]{2,1,0:T(8,128)(2,1)}), bf16[64,64,1536]{2,1,0:T(8,128)(2,1)}, u32[]{:S(2)}, u32[]{:S(2)}) async-start(bf16[64,64,1536]{2,1,0:T(8,128)(2,1)} %stack.2), calls=%async_computation | async-start | bytes 25165824 | tf_op jit(solution)/shard_map/all_to_all | solution.py:44
  629.5 55.5 %copy-start.2 = (f32[24,64]{1,0:T(8,128)S(1)}, f32[24,64]{1,0:T(8,128)}, u32[]{:S(2)}) copy-start(f32[24,64]{1,0:T(8,128)} %param.13) | copy-start | bytes 18436
  629.5 55.5 %copy-start.3 = (f32[64]{0:T(128)S(1)}, f32[64]{0:T(128)}, u32[]{:S(2)}) copy-start(f32[64]{0:T(128)} %param.14) | copy-start | bytes 772
  629.5 55.5 %copy-start.4 = (f32[64]{0:T(128)S(1)}, f32[64]{0:T(128)}, u32[]{:S(2)}) copy-start(f32[64]{0:T(128)} %param.15) | copy-start | bytes 772
  641.9 42.9 %all-to-all-start.1 = ((f32[8,384,64]{1,2,0:T(8,128)}), f32[8,384,64]{1,2,0:T(8,128)S(1)}, u32[]{:S(2)}, u32[]{:S(2)}) async-start(f32[8,384,64]{1,2,0:T(8,128)} %bitcast.12), calls=%async_computation.1 | async-start | bytes 1572864 | tf_op jit(solution)/shard_map/all_to_all | solution.py:17
  695.0 0.6 copy-start.1
